TPU v7x, 256 devices: a whole 4x4x8 slice. The times are simulated.
256 devices in a mesh: chan: 16 (over x, y_lo, core), win: 16 (over y_hi, z).
Axes of the slice: x: 4, y: 4 (y_hi: 2, y_lo: 2; y = y_hi * 2 + y_lo), z: 8, core: 2. Of those that a mesh axis runs over, the one named last changes fastest.
Arguments:
- strain: bfloat16 [4096, 16384], P('chan', 'win'), may hold values from -6 to 6
- alive_flags: int32 [4096], P('chan'), may hold values 0 or 1
Outputs:
- correlation: float32 [4096, 2, 4096], P('win', None, 'chan')
All inputs are finite; a program needn't handle non-finite values. No bound on the sum of `alive_flags` on one device may be relied on, other than what follows from the above.
Results may differ from a plain program's by a relative error of at most 0.0059.
Values may be sent and summed in bfloat16 or wider, within the bound.
A program may use at most 128 MiB of HBM per device.

v0:
```python
import math

import jax
import jax.numpy as jnp
from jax import lax
from jax.sharding import PartitionSpec as P

NF = 256
FIRST_BIN = 64
SEG = 1024
TREND_REACH = 8
LEVEL_REACH = 32
BIN_REACH = 4
LAGS = 2


def with_halo(value, sides, width):
    for axis, dim in sides:
        devices, length = (lax.axis_size(axis), value.shape[dim])
        up = [(i, (i + 1) % devices) for i in range(devices - 1)]
        down = [(j, i) for i, j in up]
        last = lax.slice_in_dim(value, length - width, length, axis=dim)
        leading = lax.slice_in_dim(value, 0, width, axis=dim)
        before = lax.ppermute(last, axis, up)
        after = lax.ppermute(leading, axis, down)
        value = jnp.concatenate([before, value, after], axis=dim)
    return value


def window_sum(values, window_len):
    window_dims = (1,) * (values.ndim - 1) + (window_len,)
    return lax.reduce_window(
        values, jnp.zeros((), values.dtype), lax.add, window_dims, (1,) * values.ndim, "VALID"
    )


def condition(padded, trend_reach, level_reach):
    padded_len = padded.shape[-1]
    trend_mean = window_sum(padded, 2 * trend_reach + 1) / (2 * trend_reach + 1)
    detrended = padded[:, trend_reach : padded_len - trend_reach] - trend_mean
    inner_len = detrended.shape[-1]
    level_mean = window_sum(jnp.abs(detrended), 2 * level_reach + 1) / (2 * level_reach + 1)
    return detrended[:, level_reach : inner_len - level_reach] / (level_mean + 1e-05)


def dft_table(seg_len, bin_count, first_bin):
    sample_idx = jnp.arange(seg_len, dtype=jnp.int32)[:, None]
    bin_idx = jnp.arange(bin_count, dtype=jnp.int32)[None, :] + first_bin
    phase_angle = 2.0 * math.pi / seg_len * (sample_idx * bin_idx % seg_len).astype(jnp.float32)
    return jnp.concatenate([jnp.cos(phase_angle), -jnp.sin(phase_angle)], axis=1).astype(
        jnp.bfloat16
    )


def lag_tables(seg_len, bin_count, first_bin, lag_count):
    lag_idx = jnp.arange(lag_count, dtype=jnp.int32)[:, None]
    lag_shift = 2 * (2 * lag_idx - lag_count + 1)
    bin_idx = jnp.arange(bin_count, dtype=jnp.int32)[None, :] + first_bin
    phase_angle = 2.0 * math.pi / seg_len * (bin_idx * lag_shift % seg_len).astype(jnp.float32)
    return (jnp.cos(phase_angle), jnp.sin(phase_angle))


def whiten(spectra, alive_col, bin_count, bin_reach):
    real_part = spectra[..., :bin_count]
    imag_part = spectra[..., bin_count:]
    magnitude = jnp.sqrt(real_part * real_part + imag_part * imag_part)
    pad_spec = ((0, 0),) * (magnitude.ndim - 1) + ((bin_reach, bin_reach),)
    smoothed = window_sum(jnp.pad(magnitude, pad_spec), 2 * bin_reach + 1) / (2 * bin_reach + 1)
    level_mean = jnp.mean(magnitude, axis=-1, keepdims=True)
    factor = alive_col / (smoothed + level_mean + 1e-05)
    return jnp.concatenate([real_part * factor, imag_part * factor], axis=-1).astype(jnp.bfloat16)


def rotate(panel, lag_cos, lag_sin, bin_count):
    row_count = panel.shape[0]
    split_parts = panel.astype(jnp.float32).reshape(row_count, -1, 2, bin_count)
    real_part = split_parts[None, :, :, 0, :]
    imag_part = split_parts[None, :, :, 1, :]
    cosine = lag_cos[:, None, None, :]
    sine_part = lag_sin[:, None, None, :]
    turned = jnp.stack(
        [real_part * cosine + imag_part * sine_part, imag_part * cosine - real_part * sine_part],
        axis=3,
    )
    return turned.reshape(lag_cos.shape[0], row_count, -1).astype(jnp.bfloat16)


def local(strain, alive_flags):
    margin = TREND_REACH + LEVEL_REACH
    padded = with_halo(strain, (("win", 1),), margin)
    normal = condition(padded.astype(jnp.float32), TREND_REACH, LEVEL_REACH)
    spectra = jnp.dot(
        normal.astype(jnp.bfloat16),
        dft_table(SEG, NF, FIRST_BIN),
        preferred_element_type=jnp.float32,
    )
    white = whiten(spectra, alive_flags.astype(jnp.float32)[:, None], NF, BIN_REACH)
    lag_cos, lag_sin = lag_tables(SEG, NF, FIRST_BIN, LAGS)
    stack_scale = 1.0 / math.sqrt(NF * lax.axis_size("win"))
    turned = rotate(lax.all_gather(white, "chan", axis=0, tiled=True), lag_cos, lag_sin, NF)
    running = jnp.einsum("lkf,cf->klc", turned, white, preferred_element_type=jnp.float32)
    stacked = lax.psum_scatter(running, "win", scatter_dimension=0, tiled=True)
    return stacked * stack_scale


def solution(mesh):
    return jax.shard_map(
        local,
        mesh=mesh,
        in_specs=(P("chan", "win"), P("chan")),
        out_specs=P("win", None, "chan"),
        check_vma=False,
    )
```

profile of v0, /device:TPU:1, one launch (start us, length us, event | category | flops | bytes accessed | tf_op | source)
XLA Modules:
  0.0 408.8 jit_solution(17457505376964404302)
XLA Ops:
  6.5 0.0 all-gather.2.cloned.1.call-start
  6.5 1.2 copy.3
  7.8 4.4 %collective-permute-start = (bf16[256,40]{0,1:T(8,128)(2,1)S(1)}, bf16[256,40]{0,1:T(8,128)(2,1)S(1)}, u32[]{:S(2)}, u32[]{:S(2)}) collective-permute-start(bf16[256,40]{0,1:T(8,128)(2,1)S(1)} %get-tuple-element.15), channel_id=1, source_target_pairs={{0,1},{1,2},{2,3},{3,4},{4,5},{5,6},{6,7},{7,8},{8,9},{9,10},{10,1... | collective-permute-start | bytes 61448 | tf_op jit(solution)/shard_map/ppermute | solution.py:24
  12.2 1.3 collective-permute-start.1
  13.5 5.0 %cosine_convert_fusion = (bf16[1024,256]{1,0:T(8,128)(2,1)}, bf16[1024,256]{1,0:T(8,128)(2,1)}) fusion(s32[256]{0:T(256)S(1)} %iota_add_fusion), kind=kLoop, calls=%fused_computation.20 | loop fusion | flops 4456448 | bytes 1049600 | tf_op jit(solution)/shard_map/convert.5
  18.5 0.7 convert_element_type.42
  19.2 0.0 collective-permute-done
  19.2 0.0 collective-permute-done.1
  19.2 0.1 maximum_convert_fusion
  19.3 5.2 %reduce_window.21 = f32[256,1088]{0,1:T(8,128)S(1)} reduce-window(f32[256,1104]{0,1:T(8,128)S(1)} %maximum_convert_fusion, f32[]{:T(128)} %constant.23.clone.1), window={size=1x17}, to_apply=%region_0.0 | reduce-window | flops 4456448 | bytes 2244612 | tf_op jit(solution)/shard_map/reduce_window | solution.py:32
  24.5 1.2 fusion.24
  25.7 18.2 %reduce_window.22 = f32[256,1024]{0,1:T(8,128)S(1)} reduce-window(f32[256,1088]{0,1:T(8,128)S(1)} %get-tuple-element.7, f32[]{:T(128)} %constant.23.clone.1), window={size=1x65}, to_apply=%region_1.0 | reduce-window | flops 16777216 | bytes 2162692 | tf_op jit(solution)/shard_map/reduce_window | solution.py:32
  43.9 2.0 fusion.4
  45.9 0.2 fusion.23
  46.0 0.9 reduce_window.23
  46.9 0.1 multiply_convert_fusion.1
  47.1 0.7 pad_maximum_fusion.1
  47.8 0.0 all-gather.2.cloned.1.call-update
  47.8 0.0 reduce-scatter.2.cloned.1.call-start
  47.9 0.1 fusion.19
  48.0 45.4 %all-gather.2.cloned.1.call-done = bf16[4096,512]{1,0:T(8,128)(2,1)} async-done(((bf16[256,512]{1,0:T(8,128)(2,1)}), bf16[4096,512]{1,0:T(8,128)(2,1)}) %all-gather.2.cloned.1.call-update) | async-done | bytes 4194320 | tf_op jit(solution)/shard_map/all_gather | solution.py:100
  93.4 9.6 %reshape.125 = f32[4096,1,2,256]{3,2,0,1:T(2,128)} reshape(bf16[4096,512]{1,0:T(8,128)(2,1)} %all-gather.2.cloned.1.call-done) | data formatting | bytes 12582912 | tf_op jit(solution)/shard_map/reshape | solution.py:76
  103.0 9.8 %fusion.25 = (f32[4096,1,1,256]{3,2,0,1:T(1,128)S(1)}, f32[4096,1,1,256]{3,2,0,1:T(1,128)S(1)}) fusion(f32[4096,1,2,256]{3,2,0,1:T(2,128)} %reshape.125), kind=kLoop, calls=%fused_computation.51 | loop fusion | bytes 16777216 | tf_op jit(solution)/shard_map/slice | solution.py:77
  112.9 2.5 copy_bitcast_fusion
  115.3 20.0 %add_convert_fusion = (bf16[2,4096,1,1,256]{4,3,1,0,2:T(2,128)(2,1)}, bf16[2,4096,1,1,256]{4,3,1,0,2:T(2,128)(2,1)}) fusion(f32[2,256]{1,0:T(2,128)S(1)} %get-tuple-element.18, f32[4096,256]{1,0:T(8,128)S(1)} %get-tuple-element.21, f32[2,256]{1,0:T(2,128)S(1)} %get-tuple-element.17, f32[4096,256]{1,0:T(8,128)} %get-tuple-element.22), kind=kLoop, calls=%fused_computation.2 | loop fusion | flops 16777216 | bytes 16781312 | tf_op jit(solution)/shard_map/convert.1
  135.3 19.9 %pad_maximum_fusion = bf16[2,4096,1,2,256]{4,3,1,0,2:T(2,128)(2,1)} fusion(bf16[2,4096,1,1,256]{4,3,1,0,2:T(2,128)(2,1)} %get-tuple-element.10, bf16[2,4096,1,1,256]{4,3,1,0,2:T(2,128)(2,1)} %get-tuple-element.9), kind=kLoop, calls=%fused_computation | loop fusion | flops 16777216 | bytes 16777216 | tf_op jit(solution)/shard_map/stack | solution.py:81
  155.2 14.1 %convert_element_type.44 = bf16[2,4096,512]{2,1,0:T(8,128)(2,1)} reshape(bf16[2,4096,1,2,256]{4,3,1,0,2:T(2,128)(2,1)} %pad_maximum_fusion) | data formatting | bytes 16777216 | tf_op jit(solution)/shard_map/convert_element_type | solution.py:85
  169.3 9.0 %convolution_bitcast_fusion = f32[4096,2,256]{0,2,1:T(8,128)} fusion(bf16[2,4096,512]{2,1,0:T(8,128)(2,1)} %convert_element_type.44, bf16[256,256]{1,0:T(8,128)(2,1)S(1)} %get-tuple-element.14, bf16[256,256]{1,0:T(8,128)(2,1)S(1)} %get-tuple-element.13), kind=kOutput, calls=%fused_computation.3 | convolution fusion | flops 2148007936 | bytes 17039360 | tf_op jit(solution)/shard_map/lkf,cf->klc/dot_general | solution.py:101
  178.3 0.0 reduce-scatter.2.cloned.1.call-update
  178.3 221.5 %reduce-scatter.2.cloned.1.call-done = f32[256,2,256]{0,2,1:T(8,128)} async-done(((f32[4096,2,256]{0,2,1:T(8,128)}), f32[256,2,256]{0,2,1:T(8,128)}) %reduce-scatter.2.cloned.1.call-update) | async-done | bytes 524304 | tf_op jit(solution)/shard_map/reduce_scatter | solution.py:102
  399.9 1.1 broadcast_multiply_fusion
  400.9 1.0 copy.6
  (4 shorter events, 0.0 us)
Async XLA Ops:
  6.5 86.9 %all-gather.2.cloned.1.call-start = ((), (), s32[]{:S(2)}) async-start(), calls=%async_computation.1 | async-start | bytes 4456448 | tf_op jit(solution)/shard_map/all_gather | solution.py:100
  7.8 11.4 %collective-permute-start = (bf16[256,40]{0,1:T(8,128)(2,1)S(1)}, bf16[256,40]{0,1:T(8,128)(2,1)S(1)}, u32[]{:S(2)}, u32[]{:S(2)}) collective-permute-start(bf16[256,40]{0,1:T(8,128)(2,1)S(1)} %get-tuple-element.15), channel_id=1, source_target_pairs={{0,1},{1,2},{2,3},{3,4},{4,5},{5,6},{6,7},{7,8},{8,9},{9,10},{10,1... | collective-permute-start | bytes 61448 | tf_op jit(solution)/shard_map/ppermute | solution.py:24
  12.2 7.0 %collective-permute-start.1 = (bf16[256,40]{0,1:T(8,128)(2,1)S(1)}, bf16[256,40]{0,1:T(8,128)(2,1)S(1)}, u32[]{:S(2)}, u32[]{:S(2)}) collective-permute-start(bf16[256,40]{0,1:T(8,128)(2,1)S(1)} %get-tuple-element.16), channel_id=1, source_target_pairs={{1,0},{2,1},{3,2},{4,3},{5,4},{6,5},{7,6},{8,7},{9,8},{10,9},{11,1... | collective-permute-start | bytes 61448 | tf_op jit(solution)/shard_map/ppermute | solution.py:25
  47.8 352.0 %reduce-scatter.2.cloned.1.call-start = ((), (), s32[]{:S(2)}) async-start(), calls=%async_computation.2 | async-start | bytes 8912896 | tf_op jit(solution)/shard_map/reduce_scatter | solution.py:102
Sparse Core Ops, SparseCore 0:
  47.9 45.4 all-gather.1
  178.4 221.3 reduce-scatter.1
where the time goes:
time: 413 us; the launch traced here: 409 us
  waiting for transfers between devices  267 us (65%)
  other arithmetic  73.4 us (18%)
  local copies, waits for them, and re-layouts  38.2 us (9%)
  between operations  13.5 us (3%)
  matrix products  11 us (3%)
  starting transfers between devices  5.71 us (1%)
    reduce_scatter x1, waiting for transfers between devices, local(): stacked = lax.psum_scatter(running, 'win', scatter_dimension=0, tiled=True)  222 us
    all_gather x1, waiting for transfers between devices, local(): lax.all_gather(white, 'chan', axis=0, tiled=True)  45.4 us
    another operation x3, other arithmetic  25.2 us
    another operation x3, other arithmetic, window_sum(): lax.reduce_window(values, jnp.zeros((), values.dtype), lax.add, window_di...  24.2 us
    another operation x1, other arithmetic, rotate(): jnp.stack([real_part * cosine + imag_part * sine_part, imag_part * cosine...  19.9 us
    convert_element_type x1, local copies, waits for them, and re-layouts, rotate(): return turned.reshape(lag_cos.shape[0], row_count, -1).astype(jnp.bfloat16)  14.1 us
    slice x1, local copies, waits for them, and re-layouts, rotate(): real_part = split_parts[None, :, :, 0, :]  9.8 us
    reshape x1, local copies, waits for them, and re-layouts, rotate(): split_parts = panel.astype(jnp.float32).reshape(row_count, -1, 2, bin_count)  9.61 us
  transfers between devices with their start and end apart: 4, of which 2 were waited for; matrix products, arithmetic and copies ran while one was open for 1% of the time, Pallas kernels for 0%

commit v1 on v0

v1 whole, which is shorter than its diff:
```python
import functools
import math

import jax
import jax.numpy as jnp
import ml_dtypes
import numpy as np
from jax import lax
from jax.experimental import pallas as pl
from jax.experimental.pallas import tpu as pltpu
from jax.sharding import PartitionSpec as P

NF = 256
FIRST_BIN = 64
SEG = 1024
TREND_REACH = 8
LEVEL_REACH = 32
BIN_REACH = 4
LAGS = 2
MESH = pl.DeviceIdType.MESH

TREND = 2 * TREND_REACH + 1
LEVEL = 2 * LEVEL_REACH + 1
SMOOTH = 2 * BIN_REACH + 1
STEPS = 8
DEEPEST = 3


def constants():
    bf16 = ml_dtypes.bfloat16
    off = np.arange(512)[:, None] - 128 - np.arange(256)[None, :]
    trend = TREND * (off == 0) - 1.0 * (np.abs(off) <= TREND_REACH)
    level = 1.0 * (np.abs(off) <= LEVEL_REACH)
    k = np.arange(SEG)[:, None]
    f = np.arange(NF)[None, :] + FIRST_BIN
    angle = 2.0 * math.pi / SEG * (k * f % SEG)
    table = np.concatenate([np.cos(angle), -np.sin(angle)], axis=1)
    bins = np.arange(NF)
    near = 1.0 * (np.abs(bins[:, None] - bins[None, :]) <= BIN_REACH)
    smooth = np.concatenate([near, np.ones((NF, NF))], axis=1)
    theta = 2.0 * math.pi / SEG * (f * 2 % SEG)
    turn = np.concatenate([np.cos(theta), np.sin(theta)], axis=0)
    turn = np.concatenate([turn, np.zeros((6, NF))], axis=0)
    return (
        trend.astype(bf16),
        level.astype(bf16),
        table.astype(bf16),
        smooth.astype(bf16),
        turn.astype(np.float32),
    )


def dot(a, b):
    return jnp.dot(a, b, preferred_element_type=jnp.float32)


def kernel(
    scale,
    x_ref, alive_ref, trend_ref, level_ref, table_ref, smooth_ref, turn_ref,
    out_ref,
    halo, cbuf, kbuf, rot, acc, part_out, part_in,
    halo_send, halo_recv, c_send, c_recv, k_send, k_recv, part_send, part_recv,
):
    rows = x_ref.shape[0]
    half = rows // 2
    chan = lax.axis_index("chan")
    win = lax.axis_index("win")
    x, yl, co = chan // 4, (chan // 2) % 2, chan % 2
    yh, z = win // 8, win % 8
    z2, z1, z0 = z // 4, (z // 2) % 2, z % 2

    chan_xp = ((x + 1) % 4) * 4 + yl * 2 + co
    chan_xm = ((x + 3) % 4) * 4 + yl * 2 + co
    chan_yo = x * 4 + (1 - yl) * 2 + co
    chan_co = x * 4 + yl * 2 + (1 - co)
    win_r = yh * 8 + (z + 1) % 8
    win_l = yh * 8 + (z + 7) % 8
    win_other = (1 - yh) * 8 + z
    win_next = (win + 1) % 16
    win_prev = (win + 15) % 16

    barrier = pltpu.get_barrier_semaphore()
    for device in (
        (chan, win_r), (chan, win_l), (chan, win_next), (chan, win_prev), (chan, win_other),
        (chan_xp, win), (chan_xm, win), (chan_yo, win), (chan_co, win),
    ):
        pl.semaphore_signal(barrier, inc=1, device_id=device, device_id_type=MESH)
    pl.semaphore_wait(barrier, 9)

    to_next = pltpu.make_async_remote_copy(
        src_ref=x_ref.at[:, SEG - 128 : SEG], dst_ref=halo.at[0],
        send_sem=halo_send.at[0], recv_sem=halo_recv.at[0],
        device_id=(chan, win_next), device_id_type=MESH,
    )
    to_prev = pltpu.make_async_remote_copy(
        src_ref=x_ref.at[:, 0:128], dst_ref=halo.at[1],
        send_sem=halo_send.at[1], recv_sem=halo_recv.at[1],
        device_id=(chan, win_prev), device_id_type=MESH,
    )

    @pl.when(win < 15)
    def _():
        to_next.start()

    @pl.when(win > 0)
    def _():
        to_prev.start()

    acc[...] = jnp.zeros_like(acc)

    @pl.when(win > 0)
    def _():
        to_next.wait_recv()

    @pl.when(win == 0)
    def _():
        halo[0] = jnp.zeros_like(halo[0])

    @pl.when(win < 15)
    def _():
        to_prev.wait_recv()

    @pl.when(win == 15)
    def _():
        halo[1] = jnp.zeros_like(halo[1])

    def whiten(h):
        here = pl.ds(h * half, half)
        lines = x_ref[here, :]
        pieces = [
            dot(halo[0, here, :], trend_ref[128:256, :]) + dot(lines[:, 0:256], trend_ref[256:512, :])
        ]
        for p in range(3):
            pieces.append(dot(lines[:, 256 * p : 256 * p + 512], trend_ref[...]))
        pieces.append(
            dot(lines[:, 768:1024], trend_ref[0:256, :]) + dot(halo[1, here, :], trend_ref[256:384, :])
        )
        detrended = jnp.concatenate(pieces, axis=1)
        size = jnp.abs(detrended)
        high = size.astype(jnp.bfloat16)
        low = (size - high.astype(jnp.float32)).astype(jnp.bfloat16)
        spectra = jnp.zeros((half, 2 * NF), jnp.float32)
        for q in range(4):
            window = slice(256 * q, 256 * q + 512)
            total = dot(high[:, window], level_ref[...]) + dot(low[:, window], level_ref[...])
            middle = detrended[:, 128 + 256 * q : 384 + 256 * q]
            normal = middle * float(LEVEL) / (total + float(LEVEL * TREND * 1e-05))
            spectra += dot(normal.astype(jnp.bfloat16), table_ref[256 * q : 256 * q + 256, :])
        re, im = spectra[:, :NF], spectra[:, NF:]
        size = jnp.sqrt(re * re + im * im)
        high = size.astype(jnp.bfloat16)
        low = (size - high.astype(jnp.float32)).astype(jnp.bfloat16)
        sums = dot(high, smooth_ref[...]) + dot(low, smooth_ref[...])
        level = sums[:, :NF] * (1.0 / SMOOTH) + sums[:, NF:] * (1.0 / NF) + 1e-05
        factor = alive_ref[here, :] / level
        white = jnp.concatenate([re * factor, im * factor], axis=1)
        cbuf[0, h] = white.astype(jnp.bfloat16)

    def ring(p, u, v, h=None):
        source = cbuf.at[u, p if h is None else h]
        return pltpu.make_async_remote_copy(
            src_ref=source, dst_ref=cbuf.at[v, p],
            send_sem=c_send.at[v, p], recv_sem=c_recv.at[v, p],
            device_id=(chan, (win_r, win_l)[p]), device_id_type=MESH,
        )

    targets = (chan_co, chan_xp, chan_xm, chan_yo)

    def spread(source, s, n, p, target):
        return pltpu.make_async_remote_copy(
            src_ref=source, dst_ref=kbuf.at[s, n, p],
            send_sem=k_send.at[s, n, p, target], recv_sem=k_recv.at[s, n, p],
            device_id=(targets[target], win), device_id_type=MESH,
        )

    dy, dc = (yl + z1) % 2, (co + z0) % 2
    dx = [(x - ((s + yh) % 2) * 2 - z2 + 4) % 4 for s in range(2)]
    away = [d * (4 - d) for d in dx]
    depth = [a // 3 + a // 4 + dy for a in away]
    relays = dc == 0
    is_source = [jnp.logical_and(relays, depth[s] == 0) for s in range(2)]

    def sends(s, p):
        plus = dx[s] == 0
        minus = dx[s] == 0
        if p == 0:
            plus = jnp.logical_or(plus, dx[s] == 1)
        else:
            minus = jnp.logical_or(minus, dx[s] == 3)
        up = jnp.logical_and(dx[s] == 0, dy == 0)
        return (relays, *(jnp.logical_and(relays, c) for c in (plus, minus, up)))

    def pass_on(source, s, n, p):
        for target, wanted in enumerate(sends(s, p)):
            @pl.when(wanted)
            def _():
                spread(source, s, n, p, target).start()

    def own(s, u, p):
        return pltpu.make_async_copy(cbuf.at[u, p], kbuf.at[s, u, p], k_recv.at[s, u, p])

    def arrived(s, n, p):
        pltpu.make_async_copy(kbuf.at[s, n, p], kbuf.at[s, n, p], k_recv.at[s, n, p]).wait()

    def source_step(u, p):
        for s in range(2):
            @pl.when(is_source[s])
            def _():
                pass_on(cbuf.at[u, p], s, u, p)
                own(s, u, p).start()

    def relay_step(u):
        for p in range(2):
            for s in range(2):
                n = u - depth[s]

                @pl.when((n >= 0) & (n < STEPS) & relays & (depth[s] > 0))
                def _():
                    arrived(s, n, p)
                    pass_on(kbuf.at[s, n, p], s, n, p)

    def ready(m):
        for p in range(2):
            for s in range(2):
                @pl.when(jnp.logical_or(jnp.logical_not(relays), is_source[s]))
                def _():
                    arrived(s, m, p)

    cos, sin = turn_ref[0:1, :], turn_ref[1:2, :]

    def correlate(places):
        for h, (u, p) in enumerate(places):
            block = cbuf[u, p].astype(jnp.float32)
            re, im = block[:, :NF], block[:, NF:]
            rc, rs, ic, iss = re * cos, re * sin, im * cos, im * sin
            for lag, (a, b) in enumerate(((rc + iss, ic - rs), (rc - iss, ic + rs))):
                rot[pl.ds(lag * rows + h * half, half), :NF] = a.astype(jnp.bfloat16)
                rot[pl.ds(lag * rows + h * half, half), NF:] = b.astype(jnp.bfloat16)
        for s in (1, 0):
            for h, (u, p) in enumerate(places):
                acc[s, pl.ds(h * half, half), :] += lax.dot_general(
                    kbuf[s, u, p], rot[...], (((1,), (1,)), ((), ())),
                    preferred_element_type=jnp.float32,
                )

    for u in range(STEPS + DEEPEST):
        if u == 0:
            for h in range(2):
                whiten(h)
                ring(0, 0, 1 + h, h).start()
                ring(1, 0, 1 + h, h).start()
                source_step(0, h)
        elif u < STEPS:
            for p in range(2):
                ring(p, 0, u).wait_recv()
                if u < 5:
                    ring(p, u, u + 2).start()
                elif u == 5 + p:
                    ring(p, u, 7).start()
                source_step(u, p)
        relay_step(u)
        m = u - DEEPEST
        if m >= 0:
            ready(m)
            if m in (0, 7):
                correlate([(m, 0), (m, 1)])
            elif m % 2 == 0:
                for p in range(2):
                    correlate([(m - 1, p), (m, p)])

    part_out[...] = acc[1].astype(jnp.bfloat16)
    partial = pltpu.make_async_remote_copy(
        src_ref=part_out, dst_ref=part_in, send_sem=part_send, recv_sem=part_recv,
        device_id=(chan, win_other), device_id_type=MESH,
    )
    partial.start()

    @pl.when(win < 15)
    def _():
        to_next.wait_send()

    @pl.when(win > 0)
    def _():
        to_prev.wait_send()

    for h in range(2):
        ring(0, 0, 1 + h, h).wait_send()
        ring(1, 0, 1 + h, h).wait_send()
    for p in range(2):
        for v in range(3, STEPS):
            ring(p, 0, v).wait_send()
    for s in range(2):
        for p in range(2):
            for target, wanted in enumerate(sends(s, p)):
                @pl.when(wanted)
                def _():
                    @pl.loop(0, STEPS)
                    def _(n):
                        spread(kbuf.at[s, n, p], s, n, p, target).wait_send()
    partial.wait_send()
    partial.wait_recv()
    out_ref[...] = (acc[0] + part_in[...].astype(jnp.float32)) * scale


def local(strain, alive_flags):
    rows = strain.shape[0]
    half = rows // 2
    scale = 1.0 / math.sqrt(NF * lax.axis_size("win"))
    vmem = pl.BlockSpec(memory_space=pltpu.VMEM)
    dma = pltpu.SemaphoreType.DMA
    stacked = pl.pallas_call(
        functools.partial(kernel, scale),
        out_shape=jax.ShapeDtypeStruct((rows, LAGS * rows), jnp.float32),
        in_specs=[vmem] * 7,
        out_specs=vmem,
        scratch_shapes=[
            pltpu.VMEM((2, rows, 128), jnp.bfloat16),
            pltpu.VMEM((STEPS, 2, half, 2 * NF), jnp.bfloat16),
            pltpu.VMEM((2, STEPS, 2, half, 2 * NF), jnp.bfloat16),
            pltpu.VMEM((LAGS * rows, 2 * NF), jnp.bfloat16),
            pltpu.VMEM((2, rows, LAGS * rows), jnp.float32),
            pltpu.VMEM((rows, LAGS * rows), jnp.bfloat16),
            pltpu.VMEM((rows, LAGS * rows), jnp.bfloat16),
            dma((2,)), dma((2,)),
            dma((STEPS, 2)), dma((STEPS, 2)),
            dma((2, STEPS, 2, 4)), dma((2, STEPS, 2)),
            dma, dma,
        ],
        compiler_params=pltpu.CompilerParams(
            collective_id=0, has_side_effects=True, vmem_limit_bytes=40 * 1024 * 1024
        ),
        cost_estimate=pl.CostEstimate(
            flops=3_000_000_000, bytes_accessed=4_000_000, transcendentals=0
        ),
    )(strain, alive_flags.astype(jnp.float32)[:, None], *constants())
    return stacked.reshape(rows, LAGS, rows)


def solution(mesh):
    return jax.shard_map(
        local,
        mesh=mesh,
        in_specs=(P("chan", "win"), P("chan")),
        out_specs=P("win", None, "chan"),
        check_vma=False,
    )
```

time: 413 us -> 75.3 us (0.18)
  the two profiles are of different devices: /device:TPU:1 before, /device:TPU:25 now
where the time goes in v1:
time: 75.3 us; the launch traced here: 75 us
  Pallas kernels  67.4 us (90%)
  local copies, waits for them, and re-layouts  6.92 us (9%)
    pallas_call x1, Pallas kernels, local(): pl.pallas_call(functools.partial(kernel, scale), out_shape=jax.ShapeDtype...  67.4 us
    unnamed x12, local copies, waits for them, and re-layouts  5.67 us

profile of v1, /device:TPU:25, one launch (start us, length us, event | category | flops | bytes accessed | tf_op | source)
XLA Modules:
  0.0 75.0 jit_solution(11672003976876811107)
XLA Ops:
  0.0 0.7 convert_element_type.3
  0.7 0.0 copy-start.5
  0.7 0.1 copy.8.alive_ref
  0.8 0.6 copy-done.5
  1.4 0.0 copy-start
  1.4 1.0 %copy-done = bf16[256,1024]{1,0:T(8,128)(2,1)S(1)} copy-done((bf16[256,1024]{1,0:T(8,128)(2,1)S(1)}, bf16[256,1024]{1,0:T(8,128)(2,1)}, u32[]{:S(2)}) %copy-start) | copy-done | bytes 524312
  2.4 0.0 copy-start.1
  2.4 1.2 %copy-done.1 = bf16[1024,512]{1,0:T(8,128)(2,1)S(1)} copy-done((bf16[1024,512]{1,0:T(8,128)(2,1)S(1)}, bf16[1024,512]{1,0:T(8,128)(2,1)}, u32[]{:S(2)}) %copy-start.1) | copy-done | bytes 1048600
  3.6 0.0 copy-start.2
  3.6 0.9 %copy-done.2 = bf16[256,512]{1,0:T(8,128)(2,1)S(1)} copy-done((bf16[256,512]{1,0:T(8,128)(2,1)S(1)}, bf16[256,512]{1,0:T(8,128)(2,1)}, u32[]{:S(2)}) %copy-start.2) | copy-done | bytes 262168
  4.6 0.0 copy-start.3
  4.6 0.9 %copy-done.3 = bf16[512,256]{1,0:T(8,128)(2,1)S(1)} copy-done((bf16[512,256]{1,0:T(8,128)(2,1)S(1)}, bf16[512,256]{1,0:T(8,128)(2,1)}, u32[]{:S(2)}) %copy-start.3) | copy-done | bytes 262168
  5.5 0.0 copy-start.4
  5.5 0.9 %copy-done.4 = bf16[512,256]{1,0:T(8,128)(2,1)S(1)} copy-done((bf16[512,256]{1,0:T(8,128)(2,1)S(1)}, bf16[512,256]{1,0:T(8,128)(2,1)}, u32[]{:S(2)}) %copy-start.4) | copy-done | bytes 262168
  6.5 67.4 %shard_map.73 = f32[256,512]{1,0:T(8,128)S(1)} custom-call(bf16[256,1024]{1,0:T(8,128)(2,1)S(1)} %copy-done, f32[256,1]{1,0:T(8,128)S(1)} %copy.8.alive_ref, bf16[512,256]{1,0:T(8,128)(2,1)S(1)} %copy-done.4, bf16[512,256]{1,0:T(8,128)(2,1)S(1)} %copy-done.3, bf16[1024,512]{1,0:T(8,128)(2,1)S(1)} %copy-done.1, bf16[256,512]{1,0:T(8,128)(2,1)S(1)} %copy-done.2, ...), custom_call_target="tpu_custom_call" | custom-call | flops 3000000000 | bytes 4000000 | tf_op jit(solution)/shard_map/pallas_call | solution.py:311
  73.9 1.1 %reshape.3 = f32[256,2,256]{2,1,0:T(2,128)} reshape(f32[256,512]{1,0:T(8,128)S(1)} %shard_map.73) | data formatting | bytes 1048576 | tf_op jit(solution)/shard_map/reshape | solution.py:336
Async XLA Ops:
  0.7 0.7 copy-start.5
  1.4 1.0 %copy-start = (bf16[256,1024]{1,0:T(8,128)(2,1)S(1)}, bf16[256,1024]{1,0:T(8,128)(2,1)}, u32[]{:S(2)}) copy-start(bf16[256,1024]{1,0:T(8,128)(2,1)} %x_ref.1) | copy-start | bytes 1572868
  2.4 1.2 %copy-start.1 = (bf16[1024,512]{1,0:T(8,128)(2,1)S(1)}, bf16[1024,512]{1,0:T(8,128)(2,1)}, u32[]{:S(2)}) copy-start(bf16[1024,512]{1,0:T(8,128)(2,1)} %constant.12.clone.table_ref) | copy-start | bytes 3145732
  3.6 0.9 %copy-start.2 = (bf16[256,512]{1,0:T(8,128)(2,1)S(1)}, bf16[256,512]{1,0:T(8,128)(2,1)}, u32[]{:S(2)}) copy-start(bf16[256,512]{1,0:T(8,128)(2,1)} %constant.13.clone.smooth_ref) | copy-start | bytes 786436
  4.6 0.9 %copy-start.3 = (bf16[512,256]{1,0:T(8,128)(2,1)S(1)}, bf16[512,256]{1,0:T(8,128)(2,1)}, u32[]{:S(2)}) copy-start(bf16[512,256]{1,0:T(8,128)(2,1)} %constant.11.clone.level_ref) | copy-start | bytes 786436
  5.5 0.9 %copy-start.4 = (bf16[512,256]{1,0:T(8,128)(2,1)S(1)}, bf16[512,256]{1,0:T(8,128)(2,1)}, u32[]{:S(2)}) copy-start(bf16[512,256]{1,0:T(8,128)(2,1)} %constant.10.clone.trend_ref) | copy-start | bytes 786436

commit v2 on v1

v2 whole, which is shorter than its diff:
```python
import functools
import math

import jax
import jax.numpy as jnp
import ml_dtypes
import numpy as np
from jax import lax
from jax.experimental import pallas as pl
from jax.experimental.pallas import tpu as pltpu
from jax.sharding import PartitionSpec as P

NF = 256
FIRST_BIN = 64
SEG = 1024
TREND_REACH = 8
LEVEL_REACH = 32
BIN_REACH = 4
LAGS = 2
MESH = pl.DeviceIdType.MESH

TREND = 2 * TREND_REACH + 1
LEVEL = 2 * LEVEL_REACH + 1
SMOOTH = 2 * BIN_REACH + 1
STEPS = 8


def constants():
    bf16 = ml_dtypes.bfloat16
    off = np.arange(512)[:, None] - 128 - np.arange(256)[None, :]
    trend = TREND * (off == 0) - 1.0 * (np.abs(off) <= TREND_REACH)
    level = 1.0 * (np.abs(off) <= LEVEL_REACH)
    k = np.arange(SEG)[:, None]
    f = np.arange(NF)[None, :] + FIRST_BIN
    angle = 2.0 * math.pi / SEG * (k * f % SEG)
    table = np.concatenate([np.cos(angle), -np.sin(angle)], axis=1)
    bins = np.arange(NF)
    near = 1.0 * (np.abs(bins[:, None] - bins[None, :]) <= BIN_REACH)
    smooth = np.concatenate([near, np.ones((NF, NF))], axis=1)
    theta = 2.0 * math.pi / SEG * (f * 2 % SEG)
    turn = np.concatenate([np.cos(theta), np.sin(theta)], axis=0)
    turn = np.concatenate([turn, np.zeros((6, NF))], axis=0)
    return (
        trend.astype(bf16),
        level.astype(bf16),
        table.astype(bf16),
        smooth.astype(bf16),
        turn.astype(np.float32),
    )


def dot(a, b):
    return jnp.dot(a, b, preferred_element_type=jnp.float32)


def kernel(
    scale,
    x_hbm, alive_hbm, trend_hbm, level_hbm, table_hbm, smooth_hbm, turn_hbm,
    out_ref,
    x_ref, alive_ref, trend_ref, level_ref, table_ref, smooth_ref, turn_ref, load_sem,
    halo, cbuf, moved, kbuf, rot, acc, part_out, part_in,
    halo_send, halo_recv, c_send, c_recv, m_send, m_recv, s_send, s_recv, k_send, k_recv, part_send, part_recv,
):
    rows = x_ref.shape[0]
    half = rows // 2
    loads = [
        pltpu.make_async_copy(source, held, load_sem.at[i])
        for i, (source, held) in enumerate((
            (x_hbm, x_ref), (trend_hbm, trend_ref), (level_hbm, level_ref), (table_hbm, table_ref),
            (smooth_hbm, smooth_ref), (alive_hbm, alive_ref), (turn_hbm, turn_ref),
        ))
    ]
    for load in loads:
        load.start()
    chan = lax.axis_index("chan")
    win = lax.axis_index("win")
    x, yl, co = chan // 4, (chan // 2) % 2, chan % 2
    yh, z = win // 8, win % 8
    z2, z1, z0 = z // 4, (z // 2) % 2, z % 2

    chan_xp = ((x + 1) % 4) * 4 + yl * 2 + co
    chan_xm = ((x + 3) % 4) * 4 + yl * 2 + co
    chan_yo = x * 4 + (1 - yl) * 2 + co
    chan_co = x * 4 + yl * 2 + (1 - co)
    win_r = yh * 8 + (z + 1) % 8
    win_l = yh * 8 + (z + 7) % 8
    win_other = (1 - yh) * 8 + z
    win_next = (win + 1) % 16
    win_prev = (win + 15) % 16

    chan_x2 = ((x + 2) % 4) * 4 + yl * 2 + co
    column, pair = (chan // 2) % 4, z // 2
    base = (chan // 8) * 8

    def xor(a, b):
        return (a // 2 + b // 2) % 2 * 2 + (a + b) % 2

    via = [xor(xor(column, pair), 2 * h + co) for h in range(2)]
    via_chan = [base + 2 * via[h] + co for h in range(2)]
    moves = [via[h] != column for h in range(2)]
    swap_chan = base + 2 * column + z0
    swap_win = [yh * 8 + 2 * via[h] + co for h in range(2)]
    giver_chan = base + 2 * column + z0
    giver_win = [yh * 8 + 2 * xor(xor(column, pair), 2 * h + z0) + co for h in range(2)]
    swaps = [2 * via[h] + co != z for h in range(2)]

    barrier = pltpu.get_barrier_semaphore()
    for device in (
        (chan, win_r), (chan, win_l), (chan, win_next), (chan, win_prev), (chan, win_other),
        (chan_xp, win), (chan_xm, win), (chan_x2, win), (chan_yo, win), (chan_co, win),
    ):
        pl.semaphore_signal(barrier, inc=1, device_id=device, device_id_type=MESH)

    for h in range(2):
        @pl.when(2 * xor(xor(column, pair), 2 * h + z0) + co != z)
        def _():
            pl.semaphore_signal(barrier, inc=1, device_id=(giver_chan, giver_win[h]), device_id_type=MESH)

        @pl.when(moves[h])
        def _():
            pl.semaphore_signal(barrier, inc=1, device_id=(via_chan[h], win), device_id_type=MESH)

    pl.semaphore_wait(barrier, 10 + sum(w.astype(jnp.int32) for w in (*swaps, *moves)))

    to_next = pltpu.make_async_remote_copy(
        src_ref=x_hbm.at[:, SEG - 128 : SEG], dst_ref=halo.at[0],
        send_sem=halo_send.at[0], recv_sem=halo_recv.at[0],
        device_id=(chan, win_next), device_id_type=MESH,
    )
    to_prev = pltpu.make_async_remote_copy(
        src_ref=x_hbm.at[:, 0:128], dst_ref=halo.at[1],
        send_sem=halo_send.at[1], recv_sem=halo_recv.at[1],
        device_id=(chan, win_prev), device_id_type=MESH,
    )

    @pl.when(win < 15)
    def _():
        to_next.start()

    @pl.when(win > 0)
    def _():
        to_prev.start()

    for load in loads:
        load.wait()

    @pl.when(win > 0)
    def _():
        to_next.wait_recv()

    @pl.when(win == 0)
    def _():
        halo[0] = jnp.zeros_like(halo[0])

    @pl.when(win < 15)
    def _():
        to_prev.wait_recv()

    @pl.when(win == 15)
    def _():
        halo[1] = jnp.zeros_like(halo[1])

    def whiten(h):
        here = pl.ds(h * half, half)
        lines = x_ref[here, :]
        pieces = [
            dot(halo[0, here, :], trend_ref[128:256, :]) + dot(lines[:, 0:256], trend_ref[256:512, :])
        ]
        for p in range(3):
            pieces.append(dot(lines[:, 256 * p : 256 * p + 512], trend_ref[...]))
        pieces.append(
            dot(lines[:, 768:1024], trend_ref[0:256, :]) + dot(halo[1, here, :], trend_ref[256:384, :])
        )
        detrended = jnp.concatenate(pieces, axis=1)
        size = jnp.abs(detrended)
        high = size.astype(jnp.bfloat16)
        low = (size - high.astype(jnp.float32)).astype(jnp.bfloat16)
        spectra = jnp.zeros((half, 2 * NF), jnp.float32)
        for q in range(4):
            window = slice(256 * q, 256 * q + 512)
            total = dot(high[:, window], level_ref[...]) + dot(low[:, window], level_ref[...])
            middle = detrended[:, 128 + 256 * q : 384 + 256 * q]
            normal = middle * float(LEVEL) / (total + float(LEVEL * TREND * 1e-05))
            spectra += dot(normal.astype(jnp.bfloat16), table_ref[256 * q : 256 * q + 256, :])
        re, im = spectra[:, :NF], spectra[:, NF:]
        size = jnp.sqrt(re * re + im * im)
        high = size.astype(jnp.bfloat16)
        low = (size - high.astype(jnp.float32)).astype(jnp.bfloat16)
        sums = dot(high, smooth_ref[...]) + dot(low, smooth_ref[...])
        level = sums[:, :NF] * (1.0 / SMOOTH) + sums[:, NF:] * (1.0 / NF) + 1e-05
        flags = jnp.broadcast_to(alive_ref[h : h + 1, :], (half, half))
        place = [lax.broadcasted_iota(jnp.int32, (half, half), d) for d in range(2)]
        flags = jnp.where(place[0] == place[1], flags, 0).astype(jnp.float32)
        factor = jnp.sum(flags, axis=1, keepdims=True) / level
        white = jnp.concatenate([re * factor, im * factor], axis=1)
        cbuf[z, h] = white.astype(jnp.bfloat16)

    def ring(p, t, h):
        source = (z + (8 - t, t)[p]) % 8
        return pltpu.make_async_remote_copy(
            src_ref=cbuf.at[source, h], dst_ref=cbuf.at[source, h],
            send_sem=c_send.at[p, t, h], recv_sem=c_recv.at[source, h],
            device_id=(chan, (win_r, win_l)[p]), device_id_type=MESH,
        )

    def ring_arrived(p, t, h):
        source = (z + (8 - t, t)[p]) % 8
        here = cbuf.at[source, h]
        pltpu.make_async_copy(here, here, c_recv.at[source, h]).wait()

    def ring_step(u):
        t = (u + 1) // 2
        for p in range(2):
            h = p if t == 4 else (u + 1) % 2
            ring_arrived(p, t, h)
            if t < 3 or (t == 3 and h == p):
                ring(p, t, h).start()

    def aside(h):
        return pltpu.make_async_remote_copy(
            src_ref=cbuf.at[z, h], dst_ref=moved.at[h],
            send_sem=m_send.at[h], recv_sem=m_recv.at[h],
            device_id=(via_chan[h], win), device_id_type=MESH,
        )

    def swap(source, h):
        return pltpu.make_async_remote_copy(
            src_ref=source, dst_ref=kbuf.at[base + z, h],
            send_sem=s_send.at[h], recv_sem=s_recv.at[h],
            device_id=(swap_chan, swap_win[h]), device_id_type=MESH,
        )

    def held_by(c, h):
        return (c // 8) * 8 + 2 * xor(xor((c // 2) % 4, pair), 2 * h + z0) + c % 2

    def keep(source, h):
        return pltpu.make_async_copy(source, kbuf.at[base + z, h], s_recv.at[h])

    def onward(source, h):
        @pl.when(swaps[h])
        def _():
            swap(source, h).start()

        @pl.when(jnp.logical_not(swaps[h]))
        def _():
            keep(source, h).start()

    def row_other(c):
        return c + 2 - 4 * ((c // 2) % 2)

    def core_other(c):
        return c + 1 - 2 * (c % 2)

    blocks = (
        chan, chan_yo, chan_xp, chan_xm, chan_x2,
        row_other(chan_xp), row_other(chan_xm), row_other(chan_x2),
    )
    targets = (chan_co, chan_xp, chan_xm, chan_x2, chan_yo)

    def spread(b, h, target):
        held = kbuf.at[held_by(blocks[b], h), h]
        return pltpu.make_async_remote_copy(
            src_ref=held, dst_ref=held,
            send_sem=k_send.at[b, h, target], recv_sem=k_recv.at[blocks[b], h],
            device_id=(targets[target], win), device_id_type=MESH,
        )

    def goes_to(b, h):
        if b == 0:
            return (1, 2, 3, 4, 0)
        if b == 1:
            return (1, 2, 3, 0) if h == 0 else (0,)
        if b < 5:
            return (4, 0) if h == 1 else (0,)
        return (0,)

    def arrived(c, h):
        held = kbuf.at[held_by(c, h), h]
        pltpu.make_async_copy(held, held, k_recv.at[c, h]).wait()

    def pass_on(b, h):
        if b == 0:
            held = kbuf.at[held_by(chan, h), h]
            pltpu.make_async_copy(held, held, s_recv.at[h]).wait()
        else:
            arrived(blocks[b], h)
        for target in goes_to(b, h):
            spread(b, h, target).start()

    cos, sin = turn_ref[0:1, :], turn_ref[1:2, :]

    def turn(source):
        for h in range(2):
            block = cbuf[source, h].astype(jnp.float32)
            re, im = block[:, :NF], block[:, NF:]
            rc, rs, ic, iss = re * cos, re * sin, im * cos, im * sin
            for lag, (a, b) in enumerate(((rc + iss, ic - rs), (rc - iss, ic + rs))):
                here = pl.ds(lag * rows + h * half, half)
                rot[source, here, :NF] = a.astype(jnp.bfloat16)
                rot[source, here, NF:] = b.astype(jnp.bfloat16)

    def product(which, lag):
        total = jnp.zeros((rows, rows), jnp.float32)
        for seg in range(STEPS):
            total += lax.dot_general(
                kbuf[which * 8 + seg].reshape(rows, 2 * NF), rot[seg, pl.ds(lag * rows, rows), :],
                (((1,), (1,)), ((), ())), preferred_element_type=jnp.float32,
            )
        return total

    def partial(h):
        return pltpu.make_async_remote_copy(
            src_ref=part_out.at[h], dst_ref=part_in.at[h],
            send_sem=part_send.at[h], recv_sem=part_recv.at[h],
            device_id=(chan, win_other), device_id_type=MESH,
        )

    for h in range(2):
        whiten(h)

        @pl.when(moves[h])
        def _():
            aside(h).start()

        @pl.when(jnp.logical_not(moves[h]))
        def _():
            onward(cbuf.at[z, h], h)

        ring(0, 0, h).start()
        ring(1, 0, h).start()

    for h in range(2):
        @pl.when(moves[h])
        def _():
            aside(h).wait_recv()
            onward(moved.at[h], h)

    turn(z)
    ring_step(1)
    ring_step(2)
    turn((z + 7) % 8)
    turn((z + 1) % 8)
    pass_on(0, 0)
    pass_on(0, 1)
    ring_step(3)
    pass_on(1, 0)
    pass_on(1, 1)
    ring_step(4)
    turn((z + 6) % 8)
    turn((z + 2) % 8)
    pass_on(2, 1)
    pass_on(3, 1)
    pass_on(4, 1)
    ring_step(5)
    pass_on(2, 0)
    pass_on(3, 0)
    pass_on(4, 0)
    ring_step(6)
    turn((z + 5) % 8)
    turn((z + 3) % 8)
    pass_on(5, 0)
    pass_on(6, 0)
    pass_on(7, 0)
    ring_step(7)
    turn((z + 4) % 8)
    pass_on(5, 1)
    pass_on(6, 1)
    pass_on(7, 1)
    for h in range(2):
        for b in range(8):
            arrived(core_other(blocks[b]), h)

    for h in range(2):
        part_out[h] = product(1 - yh, h).astype(jnp.bfloat16)
        partial(h).start()
    for h in range(2):
        acc[h] = product(yh, h)

    @pl.when(win < 15)
    def _():
        to_next.wait_send()

    @pl.when(win > 0)
    def _():
        to_prev.wait_send()

    for h in range(2):
        @pl.when(swaps[h])
        def _():
            swap(moved.at[h], h).wait_send()

        @pl.when(moves[h])
        def _():
            aside(h).wait_send()

        for p in range(2):
            for t in range(4 if h == p else 3):
                ring(p, t, h).wait_send()
        for b in range(8):
            for target in goes_to(b, h):
                spread(b, h, target).wait_send()
    for h in range(2):
        partial(h).wait_send()
        partial(h).wait_recv()
        out_ref[:, pl.ds(h * rows, rows)] = (acc[h] + part_in[h].astype(jnp.float32)) * scale


def local(strain, alive_flags):
    rows = strain.shape[0]
    half = rows // 2
    scale = 1.0 / math.sqrt(NF * lax.axis_size("win"))
    vmem = pl.BlockSpec(memory_space=pltpu.VMEM)
    tables = constants()
    dma = pltpu.SemaphoreType.DMA
    stacked = pl.pallas_call(
        functools.partial(kernel, scale),
        out_shape=jax.ShapeDtypeStruct((rows, LAGS * rows), jnp.float32),
        in_specs=[pl.BlockSpec(memory_space=pltpu.HBM)] * 7,
        out_specs=vmem,
        scratch_shapes=[
            pltpu.VMEM(strain.shape, jnp.bfloat16),
            pltpu.VMEM((2, half), jnp.int32),
            *(pltpu.VMEM(t.shape, t.dtype) for t in tables),
            dma((7,)),
            pltpu.VMEM((2, rows, 128), jnp.bfloat16),
            pltpu.VMEM((STEPS, 2, half, 2 * NF), jnp.bfloat16),
            pltpu.VMEM((2, half, 2 * NF), jnp.bfloat16),
            pltpu.VMEM((2 * STEPS, 2, half, 2 * NF), jnp.bfloat16),
            pltpu.VMEM((STEPS, LAGS * rows, 2 * NF), jnp.bfloat16),
            pltpu.VMEM((LAGS, rows, rows), jnp.float32),
            pltpu.VMEM((LAGS, rows, rows), jnp.bfloat16),
            pltpu.VMEM((LAGS, rows, rows), jnp.bfloat16),
            dma((2,)), dma((2,)),
            dma((2, 4, 2)), dma((STEPS, 2)),
            dma((2,)), dma((2,)),
            dma((2,)), dma((2,)),
            dma((8, 2, 5)), dma((2 * STEPS, 2)),
            dma((2,)), dma((2,)),
        ],
        compiler_params=pltpu.CompilerParams(
            collective_id=0, has_side_effects=True, vmem_limit_bytes=63 * 1024 * 1024
        ),
        cost_estimate=pl.CostEstimate(
            flops=3_000_000_000, bytes_accessed=4_000_000, transcendentals=0
        ),
    )(strain, alive_flags.reshape(2, half), *tables)
    return stacked.reshape(rows, LAGS, rows)


def solution(mesh):
    return jax.shard_map(
        local,
        mesh=mesh,
        in_specs=(P("chan", "win"), P("chan")),
        out_specs=P("win", None, "chan"),
        check_vma=False,
    )
```

time: 75.3 us -> 64.7 us (0.86)
  the two profiles are of different devices: /device:TPU:25 before, /device:TPU:1 now
where the time goes in v2:
time: 64.7 us; the launch traced here: 64.4 us
  Pallas kernels  62.2 us (96%)
  local copies, waits for them, and re-layouts  2.16 us (3%)
    pallas_call x1, Pallas kernels, local(): pl.pallas_call(functools.partial(kernel, scale), out_shape=jax.ShapeDtype...  62.2 us
    reshape x1, local copies, waits for them, and re-layouts, local(): return stacked.reshape(rows, LAGS, rows)  2.16 us

profile of v2, /device:TPU:1, one launch (start us, length us, event | category | flops | bytes accessed | tf_op | source)
XLA Modules:
  0.0 64.4 jit_solution(14921840793310148154)
XLA Ops:
  0.0 62.2 %shard_map.73 = f32[256,512]{1,0:T(8,128)} custom-call(bf16[256,1024]{1,0:T(8,128)(2,1)} %x_hbm.1, s32[2,128]{1,0:T(2,128)} %bitcast.1, bf16[512,256]{1,0:T(8,128)(2,1)} %constant.10.clone.trend_hbm, bf16[512,256]{1,0:T(8,128)(2,1)} %constant.11.clone.level_hbm, bf16[1024,512]{1,0:T(8,128)(2,1)} %constant.12.clone.table_hbm, ...), custom_call_target="tpu_custom_call" | custom-call | flops 3000000000 | bytes 4000000 | tf_op jit(solution)/shard_map/pallas_call | solution.py:415
  62.2 2.2 %reshape.7 = f32[256,2,256]{2,1,0:T(2,128)} reshape(f32[256,512]{1,0:T(8,128)} %shard_map.73) | data formatting | bytes 1048576 | tf_op jit(solution)/shard_map/reshape | solution.py:447

commit v3 on v2

--- a/solution.py
+++ b/solution.py
@@ -144,48 +144,33 @@
     for load in loads:
         load.wait()
 
-    @pl.when(win > 0)
-    def _():
-        to_next.wait_recv()
-
-    @pl.when(win == 0)
-    def _():
-        halo[0] = jnp.zeros_like(halo[0])
-
-    @pl.when(win < 15)
-    def _():
-        to_prev.wait_recv()
-
-    @pl.when(win == 15)
-    def _():
-        halo[1] = jnp.zeros_like(halo[1])
-
-    def whiten(h):
+    def split(value):
+        high = value.astype(jnp.bfloat16)
+        return high, (value - high.astype(jnp.float32)).astype(jnp.bfloat16)
+
+    def spectra_of(pieces, q):
+        middle = jnp.concatenate(pieces, axis=1)
+        high, low = split(jnp.abs(middle))
+        total = dot(high, level_ref[...]) + dot(low, level_ref[...])
+        normal = middle[:, 128:384] * float(LEVEL) / (total + float(LEVEL * TREND * 1e-05))
+        return dot(normal.astype(jnp.bfloat16), table_ref[256 * q : 256 * q + 256, :])
+
+    def inside(h):
+        lines = x_ref[pl.ds(h * half, half), :]
+        pieces = []
+        for p in range(3):
+            both = dot(lines[:, 256 * p : 256 * p + 512], trend_ref[...])
+            pieces += [both[:, :128], both[:, 128:]]
+        return pieces, spectra_of(pieces[0:4], 1) + spectra_of(pieces[2:6], 2)
+
+    def whiten(h, pieces, spectra):
         here = pl.ds(h * half, half)
-        lines = x_ref[here, :]
-        pieces = [
-            dot(halo[0, here, :], trend_ref[128:256, :]) + dot(lines[:, 0:256], trend_ref[256:512, :])
-        ]
-        for p in range(3):
-            pieces.append(dot(lines[:, 256 * p : 256 * p + 512], trend_ref[...]))
-        pieces.append(
-            dot(lines[:, 768:1024], trend_ref[0:256, :]) + dot(halo[1, here, :], trend_ref[256:384, :])
-        )
-        detrended = jnp.concatenate(pieces, axis=1)
-        size = jnp.abs(detrended)
-        high = size.astype(jnp.bfloat16)
-        low = (size - high.astype(jnp.float32)).astype(jnp.bfloat16)
-        spectra = jnp.zeros((half, 2 * NF), jnp.float32)
-        for q in range(4):
-            window = slice(256 * q, 256 * q + 512)
-            total = dot(high[:, window], level_ref[...]) + dot(low[:, window], level_ref[...])
-            middle = detrended[:, 128 + 256 * q : 384 + 256 * q]
-            normal = middle * float(LEVEL) / (total + float(LEVEL * TREND * 1e-05))
-            spectra += dot(normal.astype(jnp.bfloat16), table_ref[256 * q : 256 * q + 256, :])
+        first = dot(halo[0, here, :], trend_ref[128:256, :]) + dot(x_ref[here, 0:256], trend_ref[256:512, :])
+        last = dot(x_ref[here, 768:1024], trend_ref[0:256, :]) + dot(halo[1, here, :], trend_ref[256:384, :])
+        spectra += spectra_of([first] + pieces[0:2], 0) + spectra_of(pieces[4:6] + [last], 3)
         re, im = spectra[:, :NF], spectra[:, NF:]
         size = jnp.sqrt(re * re + im * im)
-        high = size.astype(jnp.bfloat16)
-        low = (size - high.astype(jnp.float32)).astype(jnp.bfloat16)
+        high, low = split(size)
         sums = dot(high, smooth_ref[...]) + dot(low, smooth_ref[...])
         level = sums[:, :NF] * (1.0 / SMOOTH) + sums[:, NF:] * (1.0 / NF) + 1e-05
         flags = jnp.broadcast_to(alive_ref[h : h + 1, :], (half, half))
@@ -267,10 +252,14 @@
 
     def goes_to(b, h):
         if b == 0:
-            return (1, 2, 3, 4, 0)
+            return (1, 2, 4, 0)
         if b == 1:
             return (1, 2, 3, 0) if h == 0 else (0,)
-        if b < 5:
+        if b == 2:
+            return (2, 4, 0) if h == 1 else (0,)
+        if b == 3:
+            return (4, 0) if h == 1 else (1, 0)
+        if b == 4:
             return (4, 0) if h == 1 else (0,)
         return (0,)
 
@@ -299,12 +288,12 @@
                 rot[source, here, :NF] = a.astype(jnp.bfloat16)
                 rot[source, here, NF:] = b.astype(jnp.bfloat16)
 
-    def product(which, lag):
-        total = jnp.zeros((rows, rows), jnp.float32)
+    def product(which, h):
+        total = jnp.zeros((half, LAGS * rows), jnp.float32)
         for seg in range(STEPS):
             total += lax.dot_general(
-                kbuf[which * 8 + seg].reshape(rows, 2 * NF), rot[seg, pl.ds(lag * rows, rows), :],
-                (((1,), (1,)), ((), ())), preferred_element_type=jnp.float32,
+                kbuf[which * 8 + seg, h], rot[seg], (((1,), (1,)), ((), ())),
+                preferred_element_type=jnp.float32,
             )
         return total
 
@@ -315,8 +304,26 @@
             device_id=(chan, win_other), device_id_type=MESH,
         )
 
-    for h in range(2):
-        whiten(h)
+    begun = [inside(h) for h in range(2)]
+
+    @pl.when(win > 0)
+    def _():
+        to_next.wait_recv()
+
+    @pl.when(win == 0)
+    def _():
+        halo[0] = jnp.zeros_like(halo[0])
+
+    @pl.when(win < 15)
+    def _():
+        to_prev.wait_recv()
+
+    @pl.when(win == 15)
+    def _():
+        halo[1] = jnp.zeros_like(halo[1])
+
+    for h in range(2):
+        whiten(h, *begun[h])
 
         @pl.when(moves[h])
         def _():
@@ -337,42 +344,43 @@
 
     turn(z)
     ring_step(1)
+    pass_on(0, 0)
+    pass_on(0, 1)
     ring_step(2)
     turn((z + 7) % 8)
     turn((z + 1) % 8)
-    pass_on(0, 0)
-    pass_on(0, 1)
     ring_step(3)
+    pass_on(3, 0)
+    pass_on(2, 1)
     pass_on(1, 0)
-    pass_on(1, 1)
     ring_step(4)
     turn((z + 6) % 8)
     turn((z + 2) % 8)
-    pass_on(2, 1)
     pass_on(3, 1)
-    pass_on(4, 1)
+    pass_on(2, 0)
+    pass_on(1, 1)
     ring_step(5)
-    pass_on(2, 0)
-    pass_on(3, 0)
-    pass_on(4, 0)
     ring_step(6)
     turn((z + 5) % 8)
     turn((z + 3) % 8)
+    pass_on(4, 0)
+    pass_on(4, 1)
     pass_on(5, 0)
     pass_on(6, 0)
     pass_on(7, 0)
+    pass_on(5, 1)
+    pass_on(6, 1)
     ring_step(7)
     turn((z + 4) % 8)
-    pass_on(5, 1)
-    pass_on(6, 1)
     pass_on(7, 1)
-    for h in range(2):
+    def finish(h):
         for b in range(8):
             arrived(core_other(blocks[b]), h)
-
-    for h in range(2):
         part_out[h] = product(1 - yh, h).astype(jnp.bfloat16)
         partial(h).start()
+
+    finish(0)
+    finish(1)
     for h in range(2):
         acc[h] = product(yh, h)
 
@@ -402,7 +410,7 @@
     for h in range(2):
         partial(h).wait_send()
         partial(h).wait_recv()
-        out_ref[:, pl.ds(h * rows, rows)] = (acc[h] + part_in[h].astype(jnp.float32)) * scale
+        out_ref[pl.ds(h * half, half), :] = (acc[h] + part_in[h].astype(jnp.float32)) * scale
 
 
 def local(strain, alive_flags):
@@ -427,9 +435,9 @@
             pltpu.VMEM((2, half, 2 * NF), jnp.bfloat16),
             pltpu.VMEM((2 * STEPS, 2, half, 2 * NF), jnp.bfloat16),
             pltpu.VMEM((STEPS, LAGS * rows, 2 * NF), jnp.bfloat16),
-            pltpu.VMEM((LAGS, rows, rows), jnp.float32),
-            pltpu.VMEM((LAGS, rows, rows), jnp.bfloat16),
-            pltpu.VMEM((LAGS, rows, rows), jnp.bfloat16),
+            pltpu.VMEM((2, half, LAGS * rows), jnp.float32),
+            pltpu.VMEM((2, half, LAGS * rows), jnp.bfloat16),
+            pltpu.VMEM((2, half, LAGS * rows), jnp.bfloat16),
             dma((2,)), dma((2,)),
             dma((2, 4, 2)), dma((STEPS, 2)),
             dma((2,)), dma((2,)),

time: 64.7 us -> 61.8 us (0.955)
  Pallas kernels: 62.2 us -> 59.5 us
    pallas_call x1, Pallas kernels: 62.2 us -> 59.5 us  [local(): pl.pallas_call(functools.partial(kernel, scale), out_shape=jax.ShapeDtype...]
where the time goes in v3:
time: 61.8 us; the launch traced here: 61.7 us
  Pallas kernels  59.5 us (96%)
  local copies, waits for them, and re-layouts  2.16 us (3%)
    pallas_call x1, Pallas kernels, local(): pl.pallas_call(functools.partial(kernel, scale), out_shape=jax.ShapeDtype...  59.5 us
    reshape x1, local copies, waits for them, and re-layouts, local(): return stacked.reshape(rows, LAGS, rows)  2.16 us

profile of v3, /device:TPU:1, one launch (start us, length us, event | category | flops | bytes accessed | tf_op | source)
XLA Modules:
  0.0 61.7 jit_solution(4356166278514114535)
XLA Ops:
  0.0 59.5 %shard_map.73 = f32[256,512]{1,0:T(8,128)} custom-call(bf16[256,1024]{1,0:T(8,128)(2,1)} %x_hbm.1, s32[2,128]{1,0:T(2,128)} %bitcast.1, bf16[512,256]{1,0:T(8,128)(2,1)} %constant.10.clone.trend_hbm, bf16[512,256]{1,0:T(8,128)(2,1)} %constant.11.clone.level_hbm, bf16[1024,512]{1,0:T(8,128)(2,1)} %constant.12.clone.table_hbm, ...), custom_call_target="tpu_custom_call" | custom-call | flops 3000000000 | bytes 4000000 | tf_op jit(solution)/shard_map/pallas_call | solution.py:423
  59.5 2.2 %reshape.7 = f32[256,2,256]{2,1,0:T(2,128)} reshape(f32[256,512]{1,0:T(8,128)} %shard_map.73) | data formatting | bytes 1048576 | tf_op jit(solution)/shard_map/reshape | solution.py:455

commit v4 on v3

--- a/solution.py
+++ b/solution.py
@@ -252,16 +252,20 @@
 
     def goes_to(b, h):
         if b == 0:
-            return (1, 2, 4, 0)
+            return ((1, None), (2, None), (4, None), (0, None)) if h == 0 else ((3, None), (1, None), (2, None), (4, None), (0, None))
         if b == 1:
-            return (1, 2, 3, 0) if h == 0 else (0,)
+            return ((1, None), (2, None), (3, None), (0, None)) if h == 0 else ((0, None),)
+        if b < 5 and h == 1:
+            return ((4, None), (0, None))
         if b == 2:
-            return (2, 4, 0) if h == 1 else (0,)
+            return ((2, 1), (0, None))
         if b == 3:
-            return (4, 0) if h == 1 else (1, 0)
-        if b == 4:
-            return (4, 0) if h == 1 else (0,)
-        return (0,)
+            return ((1, 0), (0, None))
+        return ((0, None),)
+
+    def spreads(b, h):
+        for target, core in goes_to(b, h):
+            yield spread(b, h, target), True if core is None else co == core
 
     def arrived(c, h):
         held = kbuf.at[held_by(c, h), h]
@@ -273,8 +277,11 @@
             pltpu.make_async_copy(held, held, s_recv.at[h]).wait()
         else:
             arrived(blocks[b], h)
-        for target in goes_to(b, h):
-            spread(b, h, target).start()
+        for copy, wanted in spreads(b, h):
+            if wanted is True:
+                copy.start()
+            else:
+                pl.when(wanted)(copy.start)
 
     cos, sin = turn_ref[0:1, :], turn_ref[1:2, :]
 
@@ -344,35 +351,35 @@
 
     turn(z)
     ring_step(1)
+    pass_on(0, 1)
     pass_on(0, 0)
-    pass_on(0, 1)
     ring_step(2)
     turn((z + 7) % 8)
     turn((z + 1) % 8)
     ring_step(3)
-    pass_on(3, 0)
+    pass_on(1, 0)
     pass_on(2, 1)
-    pass_on(1, 0)
+    pass_on(3, 1)
     ring_step(4)
     turn((z + 6) % 8)
     turn((z + 2) % 8)
-    pass_on(3, 1)
+    pass_on(3, 0)
     pass_on(2, 0)
-    pass_on(1, 1)
+    pass_on(4, 1)
     ring_step(5)
     ring_step(6)
     turn((z + 5) % 8)
     turn((z + 3) % 8)
+    pass_on(1, 1)
     pass_on(4, 0)
-    pass_on(4, 1)
     pass_on(5, 0)
     pass_on(6, 0)
     pass_on(7, 0)
     pass_on(5, 1)
     pass_on(6, 1)
+    pass_on(7, 1)
     ring_step(7)
     turn((z + 4) % 8)
-    pass_on(7, 1)
     def finish(h):
         for b in range(8):
             arrived(core_other(blocks[b]), h)
@@ -405,8 +412,11 @@
             for t in range(4 if h == p else 3):
                 ring(p, t, h).wait_send()
         for b in range(8):
-            for target in goes_to(b, h):
-                spread(b, h, target).wait_send()
+            for copy, wanted in spreads(b, h):
+                if wanted is True:
+                    copy.wait_send()
+                else:
+                    pl.when(wanted)(copy.wait_send)
     for h in range(2):
         partial(h).wait_send()
         partial(h).wait_recv()

time: 61.8 us -> 61.4 us (level)
  no operation moved by 1% of the time
where the time goes in v4:
time: 61.4 us; the launch traced here: 61.2 us
  Pallas kernels  59.1 us (96%)
  local copies, waits for them, and re-layouts  2.16 us (4%)
    pallas_call x1, Pallas kernels, local(): pl.pallas_call(functools.partial(kernel, scale), out_shape=jax.ShapeDtype...  59.1 us
    reshape x1, local copies, waits for them, and re-layouts, local(): return stacked.reshape(rows, LAGS, rows)  2.16 us

profile of v4, /device:TPU:1, one launch (start us, length us, event | category | flops | bytes accessed | tf_op | source)
XLA Modules:
  0.0 61.2 jit_solution(7857141496572277100)
XLA Ops:
  0.0 59.1 %shard_map.73 = f32[256,512]{1,0:T(8,128)} custom-call(bf16[256,1024]{1,0:T(8,128)(2,1)} %x_hbm.1, s32[2,128]{1,0:T(2,128)} %bitcast.1, bf16[512,256]{1,0:T(8,128)(2,1)} %constant.10.clone.trend_hbm, bf16[512,256]{1,0:T(8,128)(2,1)} %constant.11.clone.level_hbm, bf16[1024,512]{1,0:T(8,128)(2,1)} %constant.12.clone.table_hbm, ...), custom_call_target="tpu_custom_call" | custom-call | flops 3000000000 | bytes 4000000 | tf_op jit(solution)/shard_map/pallas_call | solution.py:433
  59.1 2.2 %reshape.7 = f32[256,2,256]{2,1,0:T(2,128)} reshape(f32[256,512]{1,0:T(8,128)} %shard_map.73) | data formatting | bytes 1048576 | tf_op jit(solution)/shard_map/reshape | solution.py:465

commit v5 on v4

--- a/solution.py
+++ b/solution.py
@@ -70,8 +70,6 @@
             (smooth_hbm, smooth_ref), (alive_hbm, alive_ref), (turn_hbm, turn_ref),
         ))
     ]
-    for load in loads:
-        load.start()
     chan = lax.axis_index("chan")
     win = lax.axis_index("win")
     x, yl, co = chan // 4, (chan // 2) % 2, chan % 2
@@ -120,26 +118,34 @@
         def _():
             pl.semaphore_signal(barrier, inc=1, device_id=(via_chan[h], win), device_id_type=MESH)
 
+    for load in loads:
+        load.start()
     pl.semaphore_wait(barrier, 10 + sum(w.astype(jnp.int32) for w in (*swaps, *moves)))
 
-    to_next = pltpu.make_async_remote_copy(
-        src_ref=x_hbm.at[:, SEG - 128 : SEG], dst_ref=halo.at[0],
-        send_sem=halo_send.at[0], recv_sem=halo_recv.at[0],
-        device_id=(chan, win_next), device_id_type=MESH,
-    )
-    to_prev = pltpu.make_async_remote_copy(
-        src_ref=x_hbm.at[:, 0:128], dst_ref=halo.at[1],
-        send_sem=halo_send.at[1], recv_sem=halo_recv.at[1],
-        device_id=(chan, win_prev), device_id_type=MESH,
-    )
-
-    @pl.when(win < 15)
-    def _():
-        to_next.start()
-
-    @pl.when(win > 0)
-    def _():
-        to_prev.start()
+    def to_next(h):
+        here = pl.ds(h * half, half)
+        return pltpu.make_async_remote_copy(
+            src_ref=x_hbm.at[here, SEG - 128 : SEG], dst_ref=halo.at[0, here],
+            send_sem=halo_send.at[0, h], recv_sem=halo_recv.at[0, h],
+            device_id=(chan, win_next), device_id_type=MESH,
+        )
+
+    def to_prev(h):
+        here = pl.ds(h * half, half)
+        return pltpu.make_async_remote_copy(
+            src_ref=x_hbm.at[here, 0:128], dst_ref=halo.at[1, here],
+            send_sem=halo_send.at[1, h], recv_sem=halo_recv.at[1, h],
+            device_id=(chan, win_prev), device_id_type=MESH,
+        )
+
+    for h in range(2):
+        @pl.when(win < 15)
+        def _():
+            to_next(h).start()
+
+        @pl.when(win > 0)
+        def _():
+            to_prev(h).start()
 
     for load in loads:
         load.wait()
@@ -313,35 +319,36 @@
 
     begun = [inside(h) for h in range(2)]
 
-    @pl.when(win > 0)
-    def _():
-        to_next.wait_recv()
-
     @pl.when(win == 0)
     def _():
         halo[0] = jnp.zeros_like(halo[0])
 
-    @pl.when(win < 15)
-    def _():
-        to_prev.wait_recv()
-
     @pl.when(win == 15)
     def _():
         halo[1] = jnp.zeros_like(halo[1])
 
     for h in range(2):
+        @pl.when(win > 0)
+        def _():
+            to_next(h).wait_recv()
+
+        @pl.when(win < 15)
+        def _():
+            to_prev(h).wait_recv()
+
         whiten(h, *begun[h])
-
-        @pl.when(moves[h])
-        def _():
-            aside(h).start()
-
-        @pl.when(jnp.logical_not(moves[h]))
-        def _():
-            onward(cbuf.at[z, h], h)
 
         ring(0, 0, h).start()
         ring(1, 0, h).start()
+
+        @pl.when(moves[h])
+        def _():
+            aside(h).start()
+
+        @pl.when(jnp.logical_not(moves[h]))
+        def _():
+            onward(cbuf.at[z, h], h)
+
 
     for h in range(2):
         @pl.when(moves[h])
@@ -391,13 +398,14 @@
     for h in range(2):
         acc[h] = product(yh, h)
 
-    @pl.when(win < 15)
-    def _():
-        to_next.wait_send()
-
-    @pl.when(win > 0)
-    def _():
-        to_prev.wait_send()
+    for h in range(2):
+        @pl.when(win < 15)
+        def _():
+            to_next(h).wait_send()
+
+        @pl.when(win > 0)
+        def _():
+            to_prev(h).wait_send()
 
     for h in range(2):
         @pl.when(swaps[h])
@@ -448,7 +456,7 @@
             pltpu.VMEM((2, half, LAGS * rows), jnp.float32),
             pltpu.VMEM((2, half, LAGS * rows), jnp.bfloat16),
             pltpu.VMEM((2, half, LAGS * rows), jnp.bfloat16),
-            dma((2,)), dma((2,)),
+            dma((2, 2)), dma((2, 2)),
             dma((2, 4, 2)), dma((STEPS, 2)),
             dma((2,)), dma((2,)),
             dma((2,)), dma((2,)),

time: 61.4 us -> 61.4 us (level); the launches traced: 61.2 us -> 60.4 us
  Pallas kernels: 59.1 us -> 58.2 us
    pallas_call x1, Pallas kernels: 59.1 us -> 58.2 us  [local(): pl.pallas_call(functools.partial(kernel, scale), out_shape=jax.ShapeDtype...]
where the time goes in v5:
time: 61.4 us; the launch traced here: 60.4 us
  Pallas kernels  58.2 us (95%)
  local copies, waits for them, and re-layouts  2.16 us (4%)
    pallas_call x1, Pallas kernels, local(): pl.pallas_call(functools.partial(kernel, scale), out_shape=jax.ShapeDtype...  58.2 us
    reshape x1, local copies, waits for them, and re-layouts, local(): return stacked.reshape(rows, LAGS, rows)  2.16 us

profile of v5, /device:TPU:1, one launch (start us, length us, event | category | flops | bytes accessed | tf_op | source)
XLA Modules:
  0.0 60.4 jit_solution(3568252847908203086)
XLA Ops:
  0.0 58.2 %shard_map.73 = f32[256,512]{1,0:T(8,128)} custom-call(bf16[256,1024]{1,0:T(8,128)(2,1)} %x_hbm.1, s32[2,128]{1,0:T(2,128)} %bitcast.1, bf16[512,256]{1,0:T(8,128)(2,1)} %constant.10.clone.trend_hbm, bf16[512,256]{1,0:T(8,128)(2,1)} %constant.11.clone.level_hbm, bf16[1024,512]{1,0:T(8,128)(2,1)} %constant.12.clone.table_hbm, ...), custom_call_target="tpu_custom_call" | custom-call | flops 3000000000 | bytes 4000000 | tf_op jit(solution)/shard_map/pallas_call | solution.py:441
  58.2 2.2 %reshape.7 = f32[256,2,256]{2,1,0:T(2,128)} reshape(f32[256,512]{1,0:T(8,128)} %shard_map.73) | data formatting | bytes 1048576 | tf_op jit(solution)/shard_map/reshape | solution.py:473
